TPU v7x, 256 devices: a whole 4x4x8 slice. The times are simulated.
256 devices in a mesh: wide: 64 (over z, y, x_hi), narrow: 4 (over x_lo, core).
Axes of the slice: x: 4 (x_hi: 2, x_lo: 2; x = x_hi * 2 + x_lo), y: 4, z: 8, core: 2. Of those that a mesh axis runs over, the one named last changes fastest.
Arguments:
- features: bfloat16 [65536, 2048], P(('wide', 'narrow')), may hold values from -6 to 6
- projection: bfloat16 [2048, 32], replicated, may hold values from -0.125 to 0.125
- targets: float32 [65536], P(('wide', 'narrow')), may hold values from -9 to 9
Outputs:
- solution: float32 [65536], P(('wide', 'narrow'))
- residual: float32 [65536], P(('wide', 'narrow'))
All inputs are finite; a program needn't handle non-finite values.
Results may differ from a plain program's by a relative error of at most 0.0003.
Values sent between devices are 32-bit elements; how exact they have to be, the bound alone decides.
A program may use at most 64 MiB of HBM per device.

v0:
```python
import math

import jax
import jax.numpy as jnp
from jax import lax
from jax.sharding import PartitionSpec as P

ITERS = 2


noise_var = 0.5
highest = lax.Precision.HIGHEST


def kernel_block(left, left_square, right, right_square):
    cross = jnp.dot(left, right.T, precision=highest)
    distance = left_square[:, None] + right_square[None, :] - 2.0 * cross
    return jnp.exp(distance * (-2.0 / left.shape[1]))


def on_device(features, projection, targets):
    latent = jnp.dot(features, projection, preferred_element_type=jnp.float32)
    row_latent = lax.all_gather(latent, "narrow", axis=0, tiled=True)
    column_latent = lax.all_gather(latent, "wide", axis=0, tiled=True)
    row_square = jnp.sum(row_latent * row_latent, axis=1)
    column_square = jnp.sum(column_latent * column_latent, axis=1)

    def squares_sum(vector):
        return lax.psum(jnp.sum(vector * vector), ("wide", "narrow"))

    solution = jnp.zeros_like(targets)
    residual = targets
    direction = targets
    norm_now = squares_sum(residual)
    for step in range(ITERS):
        start_rows = jnp.zeros((row_latent.shape[0],), jnp.float32)
        piece = lax.all_gather(direction, "wide", axis=0, tiled=True)
        length = piece.shape[0]
        width = math.gcd(length, 1024)

        def one_turn(turn, carry):
            offset = turn * width
            slab = lax.dynamic_slice_in_dim(column_latent, offset, width, 0)
            slab_square = lax.dynamic_slice_in_dim(column_square, offset, width, 0)
            values = lax.dynamic_slice_in_dim(piece, offset, width, 0)
            tile = kernel_block(row_latent, row_square, slab, slab_square)
            return carry + jnp.dot(tile, values, precision=highest)

        partial_rows = lax.fori_loop(0, length // width, one_turn, start_rows)
        image = (
            lax.psum_scatter(partial_rows, "narrow", scatter_dimension=0, tiled=True)
            + noise_var * direction
        )
        alpha = norm_now / lax.psum(jnp.sum(direction * image), ("wide", "narrow"))
        solution = solution + alpha * direction
        residual = residual - alpha * image
        norm_next = squares_sum(residual)
        direction = residual + norm_next / norm_now * direction
        norm_now = norm_next
    return (solution, residual)


def solution(mesh):
    in_specs = (P(("wide", "narrow"), None), P(), P(("wide", "narrow")))
    out_specs = (P(("wide", "narrow")), P(("wide", "narrow")))
    return jax.shard_map(
        on_device, mesh=mesh, in_specs=in_specs, out_specs=out_specs, check_vma=False
    )
```

profile of v0, /device:TPU:1, one launch (start us, length us, event | category | flops | bytes accessed | tf_op | source)
XLA Modules:
  0.0 926.5 jit_solution(4512780215653563027)
XLA Ops:
  10.4 8.7 all_gather.12
  21.2 155.3 %all-gather = f32[64,1,256]{2,1,0:T(1,128)S(1)} all-gather(f32[1,1,256]{2,1,0:T(1,128)} %bitcast.55), channel_id=1, replica_groups=mesh['wide'=64,'narrow'=4] {'wide'}, dimensions={0}, use_global_device_ids=true | all-gather | bytes 66560 | tf_op jit(solution)/shard_map/all_gather | solution.py:37
  176.6 6.3 copy.9
  184.7 146.7 %while.28 = (s32[]{:T(128)}, f32[1024]{0:T(1024)S(1)}, f32[1024]{0:T(1024)S(1)}, f32[16384]{0:T(1024)S(1)}, f32[16384,32]{1,0:T(8,128)}, /*index=5*/f32[1024,32]...) while((s32[]{:T(128)}, f32[1024]{0:T(1024)S(1)}, ...), condition=%wide.region_5.0_spmd.clone, body=%wide.region_4.0_spmd.clone.sunk | while | flops 419432448 | bytes 9089201 | solution.py:49
  193.9 4.6 fusion.53
  203.1 4.6 fusion.53
  212.2 4.6 fusion.53
  221.4 4.6 fusion.53
  239.7 4.6 fusion.53
  248.9 4.6 fusion.53
  331.5 33.2 %all-reduce = f32[1024]{0:T(1024)S(1)} all-reduce(f32[1024]{0:T(1024)S(1)} %get-tuple-element.250), channel_id=2, replica_groups=mesh['wide'=64,'narrow'=4] {'narrow'}, use_global_device_ids=true, to_apply=%region_6.0.clone | all-reduce | flops 1024 | bytes 8192
  365.3 72.7 %all-reduce.2 = (f32[]{:T(128)}, f32[]{:T(128)}) all-reduce(f32[]{:T(128)} %get-tuple-element.329, f32[]{:T(128)} %get-tuple-element.328), channel_id=1, replica_groups=mesh['wide'=64,'narrow'=4] {'wide','narrow'}, use_global_device_ids=true, to_apply=%region_1.0 | all-reduce | flops 2 | bytes 16 | tf_op jit(solution)/shard_map/psum | solution.py:29
  440.0 73.5 %psum.30 = f32[]{:T(128)} all-reduce(f32[]{:T(128)} %get-tuple-element.360), channel_id=1, replica_groups=mesh['wide'=64,'narrow'=4] {'wide','narrow'}, use_global_device_ids=true, to_apply=%region_10.0 | all-reduce | flops 1 | bytes 8 | tf_op jit(solution)/shard_map/psum | solution.py:29
  514.9 149.5 %all-gather.1 = f32[64,1,256]{2,1,0:T(1,128)S(1)} all-gather(f32[1,1,256]{2,1,0:T(1,128)S(1)} %bitcast.56), channel_id=1, replica_groups=mesh['wide'=64,'narrow'=4] {'wide'}, dimensions={0}, use_global_device_ids=true | all-gather | bytes 66560 | tf_op jit(solution)/shard_map/all_gather | solution.py:37
  664.4 146.7 %while.29 = (s32[]{:T(128)}, f32[1024]{0:T(1024)S(1)}, f32[1024]{0:T(1024)S(1)}, f32[16384]{0:T(1024)S(1)}, f32[16384,32]{1,0:T(8,128)}, /*index=5*/f32[1024,32]...) while((s32[]{:T(128)}, f32[1024]{0:T(1024)S(1)}, ...), condition=%wide.region_12.0_spmd.clone, body=%wide.region_11.0_spmd.clone.sunk | while | flops 419432448 | bytes 9089201 | solution.py:49
  673.5 4.6 fusion.59
  682.7 4.6 fusion.59
  691.9 4.6 fusion.59
  701.0 4.6 fusion.59
  710.2 4.6 fusion.59
  719.4 4.6 fusion.59
  728.6 4.6 fusion.59
  737.7 4.6 fusion.59
  746.9 4.6 fusion.59
  756.1 4.6 fusion.59
  765.3 4.6 fusion.59
  774.4 4.6 fusion.59
  783.6 4.6 fusion.59
  792.8 4.6 fusion.59
  801.9 4.6 fusion.59
  811.1 33.5 %all-reduce.1 = f32[1024]{0:T(1024)S(1)} all-reduce(f32[1024]{0:T(1024)S(1)} %get-tuple-element.251), channel_id=3, replica_groups=mesh['wide'=64,'narrow'=4] {'narrow'}, use_global_device_ids=true, to_apply=%region_13.0.clone | all-reduce | flops 1024 | bytes 8192
  845.3 72.4 %psum.31 = f32[]{:T(128)} all-reduce(f32[]{:T(128)} %multiply_reduce_fusion.2), channel_id=1, replica_groups=mesh['wide'=64,'narrow'=4] {'wide','narrow'}, use_global_device_ids=true, to_apply=%region_15.0 | all-reduce | flops 1 | bytes 8 | tf_op jit(solution)/shard_map/psum | solution.py:54
  (158 shorter events, 204.8 us)
Async XLA Ops:
  7.2 1.2 copy-start
  7.2 169.4 %all-gather.4.cloned.1.call-start = ((), (), s32[]{:S(2)}) async-start(), calls=%async_computation | async-start | bytes 2129920 | tf_op jit(solution)/shard_map/all_gather | solution.py:24
  184.7 179.9 %copy-start.1 = (f32[256]{0:T(256)S(1)}, f32[256]{0:T(256)}, u32[]{:S(2)}) copy-start(f32[256]{0:T(256)} %param.9) | copy-start | bytes 3076
Sparse Core Ops, SparseCore 0:
  11.4 113.8 all-gather.3
where the time goes:
time: 929 us; the launch traced here: 927 us
  blocking collectives  599 us (64%)
  matrix products  294 us (32%)
  between operations  18.8 us (2%)
  local copies, waits for them, and re-layouts  9.57 us (1%)
    all_gather x2, blocking collectives, on_device(): piece = lax.all_gather(direction, 'wide', axis=0, tiled=True)  305 us
    dot_general x32, matrix products, kernel_block(): cross = jnp.dot(left, right.T, precision=highest)  148 us
    psum x2, blocking collectives, squares_sum(): return lax.psum(jnp.sum(vector * vector), ('wide', 'narrow'))  146 us
    dot_general x32, matrix products, one_turn(): return carry + jnp.dot(tile, values, precision=highest)  144 us
    psum x1, blocking collectives, on_device(): alpha = norm_now / lax.psum(jnp.sum(direction * image), ('wide', 'narrow'))  72.4 us
    unnamed x2, blocking collectives  66.7 us
  transfers between devices with their start and end apart: 1, of which 0 were waited for; matrix products, arithmetic and copies ran while one was open for 0% of the time, Pallas kernels for 0%

commit v1 on v0

v1 whole, which is shorter than its diff:
```python
import functools
import math

import jax
import jax.numpy as jnp
from jax import lax
from jax.experimental import pallas as pl
from jax.experimental.pallas import tpu as pltpu
from jax.sharding import PartitionSpec as P

MESH = pl.DeviceIdType.MESH
F32 = jnp.float32
BF16 = jnp.bfloat16

SHIFTS = (0, 1, -2, 3, -4, 5, -6, 7, 8)
PLANE = ((0, 0), (0, 1), (0, 3), (1, 0), (3, 0), (1, 1), (1, 3), (3, 1),
         (3, 3), (0, 2), (2, 0), (1, 2), (3, 2), (2, 1), (2, 3), (2, 2))
NB = 16
NC = 9
BLK = 256
PROJ = 32
ROWS = NB * BLK
COLS = NC * BLK
DEEP = 256
CHUNK = 1024
GROUP = 768
LANES = 128
SCALE = math.sqrt(4.0 / PROJ * math.log2(math.e))
NOISE = 0.5
DIAG = 1.0 + NOISE


def place():
    w = lax.axis_index("wide")
    n = lax.axis_index("narrow")
    z = w // 8
    y = (w // 2) % 4
    x = (w % 2) * 2 + n // 2
    core = n % 2
    return z * 2 + core, y, x


def device(a, y, x):
    z = a // 2
    core = a % 2
    return ((z * 4 + y) * 2 + x // 2, (x % 2) * 2 + core)


def body(feat_hbm, proj_hbm, targ_ref, sol_ref, res_ref,
         feat, proj, lat_row, lat_col, t_row, t_col, o_row, o_col,
         side_a, side_b, wide_u, tiles, row_acc, col_acc,
         rp1, cp1, rr1, cr1, rp2, cp2, rr2, cr2,
         sc_out, sc_in, load_sem, lat_send, lat_rrecv, lat_crecv,
         small_send, small_recv, o_rrecv):
    a, y, x = place()

    def along_row(j, sign):
        dy, dx = PLANE[j]
        return device(a, (y + sign * dy + 4) % 4, (x + sign * dx + 4) % 4)

    def along_col(shift):
        return device((a + shift + 32) % 16, y, x)

    def send(src, dst, ssem, rsem, where):
        pltpu.make_async_remote_copy(
            src_ref=src, dst_ref=dst, send_sem=ssem, recv_sem=rsem,
            device_id=where, device_id_type=MESH).start()

    def settle(ref, sem):
        pltpu.make_async_copy(ref, ref, sem).wait()

    load_f = pltpu.make_async_copy(feat_hbm, feat, load_sem.at[0])
    load_p = pltpu.make_async_copy(proj_hbm, proj, load_sem.at[1])
    load_f.start()
    load_p.start()

    barrier = pltpu.get_barrier_semaphore()
    for j in range(1, NB):
        pl.semaphore_signal(barrier, inc=1, device_id=along_row(j, 1), device_id_type=MESH)
    for s in range(1, 16):
        pl.semaphore_signal(barrier, inc=1, device_id=along_col(s), device_id_type=MESH)
    t_row[0] = targ_ref[...]
    t_col[0] = targ_ref[...]
    pl.semaphore_wait(barrier, 30)

    for j in range(1, NB):
        send(targ_ref, t_row.at[j], small_send.at[0], small_recv.at[0], along_row(j, -1))
    for k in range(1, NC):
        send(targ_ref, t_col.at[k], small_send.at[1], small_recv.at[1], along_col(-SHIFTS[k]))

    load_p.wait()
    load_f.wait()
    latent = lax.dot_general(proj[...], feat[...], (((1,), (1,)), ((), ())),
                             preferred_element_type=F32)
    lat_row[0] = latent * SCALE
    for k in range(1, NB):
        send(lat_row.at[0], lat_row.at[k], lat_send.at[0], lat_rrecv.at[k], along_row(k, -1))
        if k < NC:
            send(lat_row.at[0], lat_col.at[k], lat_send.at[1], lat_crecv.at[k],
                 along_col(-SHIFTS[k]))

    settle(t_row.at[pl.ds(1, NB - 1)], small_recv.at[0])
    settle(t_col.at[pl.ds(1, NC - 1)], small_recv.at[1])

    def spread(values, j):
        for h in range(BLK // LANES):
            piece = values[:, h * LANES:(h + 1) * LANES]
            wide_u[j * BLK + h * LANES:j * BLK + (h + 1) * LANES, :] = jnp.transpose(
                jnp.broadcast_to(piece, (LANES, LANES)))

    for j in range(NB):
        spread(t_row[j], j)

    def split(v):
        h = v.astype(BF16)
        rest = v - h.astype(F32)
        m = rest.astype(BF16)
        l = (rest - m.astype(F32)).astype(BF16)
        return h, m, l

    line = lax.broadcasted_iota(jnp.int32, (16, BLK), 0)

    def parts(v):
        h, m, l = split(v)
        half = jnp.sum(v * v, axis=0, keepdims=True) * -0.5
        qh, qm, ql = (jnp.broadcast_to(q.astype(F32), (16, BLK)) for q in split(half))
        return h, m, l, qh, qm, ql

    def extra(qh, qm, ql, first):
        one = jnp.where((line >= 3 - first) & (line < 6 - first), 1.0, 0.0)
        e = jnp.where(line == first, qh, jnp.where(line == first + 1, qm,
                                                   jnp.where(line == first + 2, ql, one)))
        return e.astype(BF16)

    zeros = jnp.zeros((DEEP - 6 * PROJ - 16, BLK), BF16)

    def build_a(j):
        h, m, l, qh, qm, ql = parts(lat_row[j])
        stack = jnp.concatenate([h, h, m, m, h, l, extra(qh, qm, ql, 0), zeros], axis=0)
        side_a[j * BLK:(j + 1) * BLK, :] = jnp.transpose(stack)

    def build_b(k):
        h, m, l, qh, qm, ql = parts(lat_row[0] if k == 0 else lat_col[k])
        side_b[:, k * BLK:(k + 1) * BLK] = jnp.concatenate(
            [h, m, h, m, l, h, extra(qh, qm, ql, 3), zeros], axis=0)

    def fold_rows(r, out):
        for i in range(CHUNK // LANES):
            lo = r * CHUNK + i * LANES
            sums = jnp.sum(jnp.transpose(row_acc[lo:lo + LANES, :]), axis=0, keepdims=True)
            out[lo // BLK, :, (lo % BLK):(lo % BLK) + LANES] = sums

    def send_rows(r, out, into, sem):
        for j in range(4 * r, 4 * r + 4):
            if j:
                send(out.at[j], into.at[j], small_send.at[sem], small_recv.at[sem],
                     along_row(j, 1))

    def send_cols(ks, out, into, sem):
        for k in ks:
            if k:
                send(out.at[k], into.at[k], small_send.at[sem], small_recv.at[sem],
                     along_col(SHIFTS[k]))

    have_a, have_b = set(), set()

    def step(r, c):
        for j in range(4 * r, 4 * r + 4):
            if j not in have_a:
                have_a.add(j)
                if j:
                    settle(lat_row.at[j], lat_rrecv.at[j])
                build_a(j)
        for k in range(3 * c, 3 * c + 3):
            if k not in have_b:
                have_b.add(k)
                if k:
                    settle(lat_col.at[k], lat_crecv.at[k])
                build_b(k)
        rows = slice(r * CHUNK, (r + 1) * CHUNK)
        cols = slice(c * GROUP, (c + 1) * GROUP)
        power = jnp.dot(side_a[rows, :], side_b[:, cols], preferred_element_type=F32)
        p = jnp.exp2(power)
        tiles[rows, cols] = p
        u = wide_u[rows, :]
        total = None
        for i in range(GROUP // LANES):
            lane = c * GROUP + i * LANES
            k = lane // BLK
            piece = p[:, i * LANES:(i + 1) * LANES]
            down = jnp.sum((piece * u).reshape(CHUNK // 8, 8, LANES), axis=0)
            if r == 0:
                col_acc[:, lane:lane + LANES] = down
            else:
                col_acc[:, lane:lane + LANES] += down
            if k not in (0, NC - 1):
                v = t_col[k, :, (lane % BLK):(lane % BLK) + LANES]
                total = piece * v if total is None else total + piece * v
        if c == 0:
            row_acc[rows, :] = total
        else:
            row_acc[rows, :] += total

    def fold_cols(ks, out):
        for k in ks:
            out[k] = jnp.sum(col_acc[:, k * BLK:(k + 1) * BLK], axis=0, keepdims=True)

    order = ((0, 0), (1, 0), (0, 1), (1, 1), (2, 0), (2, 1), (0, 2), (1, 2), (2, 2),
             (3, 0), (3, 1), (3, 2))
    for r, c in order:
        step(r, c)
        if r == 3:
            fold_cols(range(3 * c, 3 * c + 3), cp1)
            send_cols(range(3 * c, 3 * c + 3), cp1, cr1, 3)
        if c == 2:
            fold_rows(r, rp1)
            send_rows(r, rp1, rr1, 2)

    def gathered(rp, rr, cp, cr, own):
        settle(rr.at[pl.ds(1, NB - 1)], small_recv.at[2 if own else 4])
        settle(cr.at[pl.ds(1, NC - 1)], small_recv.at[3 if own else 5])
        total = rp[0] + cp[0]
        for j in range(1, NB):
            total = total + rr[j]
        for k in range(1, NC):
            total = total + cr[k]
        return total

    t = targ_ref[...]
    off = gathered(rp1, rr1, cp1, cr1, True) - t
    o_row[0] = off
    o_col[0] = off
    for j in range(1, NB):
        send(o_row.at[0], o_row.at[j], small_send.at[6], o_rrecv.at[j // 4], along_row(j, -1))
        if j < NC:
            send(o_row.at[0], o_col.at[j], small_send.at[7], small_recv.at[7],
                 along_col(-SHIFTS[j]))

    def halves(v):
        return v[:, :LANES] + v[:, LANES:]

    def share_rows(slot, values, sem):
        for i, v in enumerate(values):
            sc_out[slot, :, i * LANES:(i + 1) * LANES] = halves(v)
        for j in range(1, NB):
            send(sc_out.at[slot], sc_in.at[slot, j], small_send.at[sem], small_recv.at[sem],
                 along_row(j, -1))

    def summed(slot, sem):
        settle(sc_in.at[slot, pl.ds(1, NB - 1)], small_recv.at[sem])
        total = sc_out[slot]
        for j in range(1, NB):
            total = total + sc_in[slot, j]
        return total

    def share_cols(slot, total, sem):
        sc_out[slot] = total
        for s in range(1, NB):
            send(sc_out.at[slot], sc_in.at[slot, s], small_send.at[sem], small_recv.at[sem],
                 along_col(-s))

    def scalars(total):
        return [jnp.sum(total[:, i * LANES:(i + 1) * LANES], axis=1, keepdims=True)
                for i in range(3)]

    share_rows(0, (t * t, t * off, off * off), 8)

    settle(o_col.at[pl.ds(1, NC - 1)], small_recv.at[7])
    lane_v = [jnp.broadcast_to(o_col[l * LANES // BLK, :, (l * LANES) % BLK:(l * LANES) % BLK + LANES],
                               (8, LANES)) for l in range(2, 16)]
    downs = tuple(jnp.zeros((8, LANES), F32) for _ in range(COLS // LANES))
    TAKE = 64
    for r in range(4):
        lo = max(4 * r, 1)
        settle(o_row.at[pl.ds(lo, 4 * r + 4 - lo)], o_rrecv.at[r])
        for j in range(4 * r, 4 * r + 4):
            spread(o_row[j], j)

        def some(i, downs):
            start = pl.multiple_of(r * CHUNK + i * TAKE, TAKE)
            downs = list(downs)
            for g in range(TAKE // 8):
                at = pl.ds(start + g * 8, 8)
                u = wide_u[at, :]
                total = None
                for l in range(COLS // LANES):
                    piece = tiles[at, l * LANES:(l + 1) * LANES]
                    downs[l] = downs[l] + piece * u
                    if 2 <= l < 16:
                        w = piece * lane_v[l - 2]
                        total = w if total is None else total + w
                row_acc[at, :] = total
            return tuple(downs)

        downs = lax.fori_loop(0, CHUNK // TAKE, some, downs)
        fold_rows(r, rp2)
        send_rows(r, rp2, rr2, 4)
        if r == 2:
            share_cols(1, summed(0, 8), 9)

    for k in range(NC):
        cp2[k] = jnp.concatenate([jnp.sum(downs[2 * k], axis=0, keepdims=True),
                                  jnp.sum(downs[2 * k + 1], axis=0, keepdims=True)], axis=1)
    send_cols(range(NC), cp2, cr2, 5)

    quad = jnp.zeros((1, BLK), F32)
    for j in range(NB):
        quad = quad + o_row[j] * rp2[j]
    for k in range(NC):
        quad = quad + o_col[k] * cp2[k]

    s0, s1, s2 = scalars(summed(1, 9))
    below = DIAG * s0 + s1
    alpha = s0 / below
    gamma = s1 / below
    resid = gamma * t - alpha * off
    share_rows(2, (resid * resid, resid * t, quad), 10)
    product = gathered(rp2, rr2, cp2, cr2, False) - off
    share_cols(3, summed(2, 10), 11)
    n1, cross, s3 = scalars(summed(3, 11))
    beta = n1 / s0
    both = gamma + beta
    length = n1 + 2.0 * beta * cross + beta * beta * s0
    energy = (DIAG * length + both * both * s1 - 2.0 * alpha * both * s2
              + alpha * alpha * (s3 - s2))
    step2 = n1 / energy
    direction = resid + beta * t
    image = DIAG * direction + both * off - alpha * product
    sol_ref[...] = alpha * t + step2 * direction
    res_ref[...] = resid - step2 * image

    settle(t_row.at[pl.ds(1, NB - 1)], small_send.at[0])
    settle(t_col.at[pl.ds(1, NC - 1)], small_send.at[1])
    settle(lat_row.at[pl.ds(1, NB - 1)], lat_send.at[0])
    settle(lat_col.at[pl.ds(1, NC - 1)], lat_send.at[1])
    settle(rr1.at[pl.ds(1, NB - 1)], small_send.at[2])
    settle(cr1.at[pl.ds(1, NC - 1)], small_send.at[3])
    settle(rr2.at[pl.ds(1, NB - 1)], small_send.at[4])
    settle(cr2.at[pl.ds(1, NC - 1)], small_send.at[5])
    settle(o_row.at[pl.ds(1, NB - 1)], small_send.at[6])
    settle(o_col.at[pl.ds(1, NC - 1)], small_send.at[7])
    for slot in range(4):
        settle(sc_in.at[slot, pl.ds(1, NB - 1)], small_send.at[8 + slot])


def on_device(features, projection, targets):
    vm = pl.BlockSpec(memory_space=pltpu.VMEM)
    hbm = pl.BlockSpec(memory_space=pl.ANY)
    flat = jax.ShapeDtypeStruct((1, BLK), F32)
    dma = pltpu.SemaphoreType.DMA
    sol, res = pl.pallas_call(
        body,
        out_shape=(flat, flat),
        in_specs=[hbm, hbm, vm],
        out_specs=(vm, vm),
        scratch_shapes=[
            pltpu.VMEM((BLK, 2048), BF16), pltpu.VMEM((PROJ, 2048), BF16),
            pltpu.VMEM((NB, PROJ, BLK), F32), pltpu.VMEM((NC, PROJ, BLK), F32),
            pltpu.VMEM((NB, 1, BLK), F32), pltpu.VMEM((NC, 1, BLK), F32),
            pltpu.VMEM((NB, 1, BLK), F32), pltpu.VMEM((NC, 1, BLK), F32),
            pltpu.VMEM((ROWS, DEEP), BF16), pltpu.VMEM((DEEP, COLS), BF16),
            pltpu.VMEM((ROWS, LANES), F32), pltpu.VMEM((ROWS, COLS), F32),
            pltpu.VMEM((ROWS, LANES), F32), pltpu.VMEM((8, COLS), F32),
            pltpu.VMEM((NB, 1, BLK), F32), pltpu.VMEM((NC, 1, BLK), F32),
            pltpu.VMEM((NB, 1, BLK), F32), pltpu.VMEM((NC, 1, BLK), F32),
            pltpu.VMEM((NB, 1, BLK), F32), pltpu.VMEM((NC, 1, BLK), F32),
            pltpu.VMEM((NB, 1, BLK), F32), pltpu.VMEM((NC, 1, BLK), F32),
            pltpu.VMEM((4, 1, 3 * LANES), F32), pltpu.VMEM((4, NB, 1, 3 * LANES), F32),
            dma((2,)), dma((2,)), dma((NB,)), dma((NC,)),
            dma((12,)), dma((12,)), dma((4,)),
        ],
        compiler_params=pltpu.CompilerParams(
            collective_id=0, has_side_effects=True, vmem_limit_bytes=60 * 2**20),
        name="conjugate",
    )(features, projection.T, targets.reshape(1, BLK))
    return sol.reshape(BLK), res.reshape(BLK)


def solution(mesh):
    in_specs = (P(("wide", "narrow"), None), P(), P(("wide", "narrow")))
    out_specs = (P(("wide", "narrow")), P(("wide", "narrow")))
    return jax.shard_map(
        on_device, mesh=mesh, in_specs=in_specs, out_specs=out_specs, check_vma=False)
```

time: 929 us -> 58.9 us (0.06)
  blocking collectives: 599 us -> 0 us
  matrix products: 294 us -> 0 us
  Pallas kernels: 0 us -> 56.3 us
  between operations: 18.8 us -> 0.65 us
    all_gather x3 -> x0, blocking collectives: 314 us -> none  [the longest x2 305 us: on_device(): piece = lax.all_gather(direction, 'wide', axis=0, tiled=True)]
    dot_general x65 -> x0, matrix products: 294 us -> none  [the longest x32 148 us: kernel_block(): cross = jnp.dot(left, right.T, precision=highest)]
    psum x3 -> x0, blocking collectives: 219 us -> none  [the longest x2 146 us: squares_sum(): return lax.psum(jnp.sum(vector * vector), ('wide', 'narrow'))]
    unnamed x2 -> x0, blocking collectives: 66.7 us -> none
    pallas_call x0 -> x1, Pallas kernels: none -> 56.3 us  [on_device(): pl.pallas_call(body, out_shape=(flat, flat), in_specs=[hbm, hbm, vm], out...]
  transfers between devices with their start and end apart: 1 -> 0, of which waited for: 0 -> 0; matrix products, arithmetic and copies ran while one was open for 0% -> 0% of each run, Pallas kernels for 0% -> 0%
where the time goes in v1:
time: 58.9 us; the launch traced here: 58.8 us
  Pallas kernels  56.3 us (96%)
  local copies, waits for them, and re-layouts  1.86 us (3%)
  between operations  0.65 us (1%)
    pallas_call x1, Pallas kernels, on_device(): pl.pallas_call(body, out_shape=(flat, flat), in_specs=[hbm, hbm, vm], out...  56.3 us
    unnamed x6, local copies, waits for them, and re-layouts  1.86 us

profile of v1, /device:TPU:1, one launch (start us, length us, event | category | flops | bytes accessed | tf_op | source)
XLA Modules:
  0.0 58.8 jit_solution(7228300394266519529)
XLA Ops:
  0.6 56.3 %conjugate.1 = (f32[1,256]{1,0:T(1,128)}, f32[1,256]{1,0:T(1,128)}) custom-call(bf16[256,2048]{1,0:T(8,128)(2,1)} %feat_hbm.1, bf16[32,2048]{1,0:T(8,128)(2,1)} %bitcast.4, f32[1,256]{1,0:T(1,128)} %bitcast.7), custom_call_target="tpu_custom_call" | custom-call | tf_op jit(solution)/shard_map/conjugate/pallas_call | solution.py:351
  56.9 0.0 copy-start.1
  57.0 0.7 %copy-done.1 = f32[1,256]{1,0:T(1,128)S(1)} copy-done((f32[1,256]{1,0:T(1,128)S(1)}, f32[1,256]{1,0:T(1,128)}, u32[]{:S(2)}) %copy-start.1) | copy-done | bytes 1048
  57.6 0.0 copy-start
  57.6 0.6 copy.7
  58.2 0.1 copy-done
  58.2 0.6 copy.8
Async XLA Ops:
  56.9 0.7 %copy-start.1 = (f32[1,256]{1,0:T(1,128)S(1)}, f32[1,256]{1,0:T(1,128)}, u32[]{:S(2)}) copy-start(f32[1,256]{1,0:T(1,128)} %get-tuple-element.4) | copy-start | bytes 3076
  57.6 0.6 %copy-start = (f32[1,256]{1,0:T(1,128)S(1)}, f32[1,256]{1,0:T(1,128)}, u32[]{:S(2)}) copy-start(f32[1,256]{1,0:T(1,128)} %get-tuple-element.5) | copy-start | bytes 3076

commit v2 on v1

--- a/solution.py
+++ b/solution.py
@@ -30,6 +30,11 @@
 DIAG = 1.0 + NOISE
 
 
+NEAREST_LAST = sorted(
+    ((dy, dx, dc) for dy in range(4) for dx in range(4) for dc in range(2)),
+    key=lambda d: (-min(d[0], 4 - d[0]) - min(d[1], 4 - d[1]), -d[2]))
+
+
 def place():
     w = lax.axis_index("wide")
     n = lax.axis_index("narrow")
@@ -46,12 +51,12 @@
     return ((z * 4 + y) * 2 + x // 2, (x % 2) * 2 + core)
 
 
-def body(feat_hbm, proj_hbm, targ_ref, sol_ref, res_ref,
+def body(feat_hbm, proj_hbm, targ_ref, out_ref,
          feat, proj, lat_row, lat_col, t_row, t_col, o_row, o_col,
          side_a, side_b, wide_u, tiles, row_acc, col_acc,
          rp1, cp1, rr1, cr1, rp2, cp2, rr2, cr2,
          sc_out, sc_in, load_sem, lat_send, lat_rrecv, lat_crecv,
-         small_send, small_recv, o_rrecv):
+         small_send, small_recv, t_rrecv, t_crecv, o_rrecv, o_crecv):
     a, y, x = place()
 
     def along_row(j, sign):
@@ -81,35 +86,11 @@
         pl.semaphore_signal(barrier, inc=1, device_id=along_col(s), device_id_type=MESH)
     t_row[0] = targ_ref[...]
     t_col[0] = targ_ref[...]
-    pl.semaphore_wait(barrier, 30)
-
-    for j in range(1, NB):
-        send(targ_ref, t_row.at[j], small_send.at[0], small_recv.at[0], along_row(j, -1))
-    for k in range(1, NC):
-        send(targ_ref, t_col.at[k], small_send.at[1], small_recv.at[1], along_col(-SHIFTS[k]))
-
-    load_p.wait()
-    load_f.wait()
-    latent = lax.dot_general(proj[...], feat[...], (((1,), (1,)), ((), ())),
-                             preferred_element_type=F32)
-    lat_row[0] = latent * SCALE
-    for k in range(1, NB):
-        send(lat_row.at[0], lat_row.at[k], lat_send.at[0], lat_rrecv.at[k], along_row(k, -1))
-        if k < NC:
-            send(lat_row.at[0], lat_col.at[k], lat_send.at[1], lat_crecv.at[k],
-                 along_col(-SHIFTS[k]))
-
-    settle(t_row.at[pl.ds(1, NB - 1)], small_recv.at[0])
-    settle(t_col.at[pl.ds(1, NC - 1)], small_recv.at[1])
-
     def spread(values, j):
         for h in range(BLK // LANES):
             piece = values[:, h * LANES:(h + 1) * LANES]
             wide_u[j * BLK + h * LANES:j * BLK + (h + 1) * LANES, :] = jnp.transpose(
                 jnp.broadcast_to(piece, (LANES, LANES)))
-
-    for j in range(NB):
-        spread(t_row[j], j)
 
     def split(v):
         h = v.astype(BF16)
@@ -144,6 +125,27 @@
         side_b[:, k * BLK:(k + 1) * BLK] = jnp.concatenate(
             [h, m, h, m, l, h, extra(qh, qm, ql, 3), zeros], axis=0)
 
+    load_p.wait()
+    load_f.wait()
+    latent = lax.dot_general(proj[...], feat[...], (((1,), (1,)), ((), ())),
+                             preferred_element_type=F32)
+    lat_row[0] = latent * SCALE
+    build_a(0)
+    build_b(0)
+    spread(t_row[0], 0)
+    pl.semaphore_wait(barrier, 30)
+
+    for j in range(1, NB):
+        send(targ_ref, t_row.at[j], small_send.at[0], t_rrecv.at[j // 4], along_row(j, -1))
+        if j < NC:
+            send(targ_ref, t_col.at[j], small_send.at[1], t_crecv.at[j // 3],
+                 along_col(-SHIFTS[j]))
+    for j in range(1, NC):
+        send(lat_row.at[0], lat_col.at[j], lat_send.at[1], lat_crecv.at[j],
+             along_col(-SHIFTS[j]))
+    for j in range(1, NB):
+        send(lat_row.at[0], lat_row.at[j], lat_send.at[0], lat_rrecv.at[j], along_row(j, -1))
+
     def fold_rows(r, out):
         for i in range(CHUNK // LANES):
             lo = r * CHUNK + i * LANES
@@ -162,21 +164,32 @@
                 send(out.at[k], into.at[k], small_send.at[sem], small_recv.at[sem],
                      along_col(SHIFTS[k]))
 
-    have_a, have_b = set(), set()
+    seen_r, seen_c = set(), set()
+
+    def slots(i, width):
+        return range(max(width * i, 1), width * i + width)
+
+    def span(ref, i, width):
+        near = slots(i, width)
+        return ref.at[pl.ds(near[0], len(near))]
 
     def step(r, c):
-        for j in range(4 * r, 4 * r + 4):
-            if j not in have_a:
-                have_a.add(j)
-                if j:
-                    settle(lat_row.at[j], lat_rrecv.at[j])
+        first_r, first_c = r not in seen_r, c not in seen_c
+        seen_r.add(r)
+        seen_c.add(c)
+        if first_r:
+            settle(span(t_row, r, 4), t_rrecv.at[r])
+            for j in slots(r, 4):
+                spread(t_row[j], j)
+        if first_c:
+            settle(span(t_col, c, 3), t_crecv.at[c])
+            for k in slots(c, 3):
+                settle(lat_col.at[k], lat_crecv.at[k])
+                build_b(k)
+        if first_r:
+            for j in slots(r, 4):
+                settle(lat_row.at[j], lat_rrecv.at[j])
                 build_a(j)
-        for k in range(3 * c, 3 * c + 3):
-            if k not in have_b:
-                have_b.add(k)
-                if k:
-                    settle(lat_col.at[k], lat_crecv.at[k])
-                build_b(k)
         rows = slice(r * CHUNK, (r + 1) * CHUNK)
         cols = slice(c * GROUP, (c + 1) * GROUP)
         power = jnp.dot(side_a[rows, :], side_b[:, cols], preferred_element_type=F32)
@@ -189,14 +202,14 @@
             k = lane // BLK
             piece = p[:, i * LANES:(i + 1) * LANES]
             down = jnp.sum((piece * u).reshape(CHUNK // 8, 8, LANES), axis=0)
-            if r == 0:
+            if first_c:
                 col_acc[:, lane:lane + LANES] = down
             else:
                 col_acc[:, lane:lane + LANES] += down
             if k not in (0, NC - 1):
                 v = t_col[k, :, (lane % BLK):(lane % BLK) + LANES]
                 total = piece * v if total is None else total + piece * v
-        if c == 0:
+        if first_r:
             row_acc[rows, :] = total
         else:
             row_acc[rows, :] += total
@@ -205,14 +218,19 @@
         for k in ks:
             out[k] = jnp.sum(col_acc[:, k * BLK:(k + 1) * BLK], axis=0, keepdims=True)
 
-    order = ((0, 0), (1, 0), (0, 1), (1, 1), (2, 0), (2, 1), (0, 2), (1, 2), (2, 2),
-             (3, 0), (3, 1), (3, 2))
-    for r, c in order:
+    def finish(order, i):
+        r, c = order[i]
+        later = order[i + 1:]
+        return (all(r != q for q, _ in later), all(c != q for _, q in later))
+
+    order = ((0, 0), (1, 0), (2, 0), (3, 0), (0, 1), (1, 1), (2, 1), (3, 1), (0, 2), (1, 2), (2, 2), (3, 2))
+    for i, (r, c) in enumerate(order):
         step(r, c)
-        if r == 3:
+        end_r, end_c = finish(order, i)
+        if end_c:
             fold_cols(range(3 * c, 3 * c + 3), cp1)
             send_cols(range(3 * c, 3 * c + 3), cp1, cr1, 3)
-        if c == 2:
+        if end_r:
             fold_rows(r, rp1)
             send_rows(r, rp1, rr1, 2)
 
@@ -228,51 +246,63 @@
 
     t = targ_ref[...]
     off = gathered(rp1, rr1, cp1, cr1, True) - t
+    def halves(v):
+        return v[:, :LANES] + v[:, LANES:]
+
     o_row[0] = off
     o_col[0] = off
     for j in range(1, NB):
         send(o_row.at[0], o_row.at[j], small_send.at[6], o_rrecv.at[j // 4], along_row(j, -1))
         if j < NC:
-            send(o_row.at[0], o_col.at[j], small_send.at[7], small_recv.at[7],
+            send(o_col.at[0], o_col.at[j], small_send.at[7], o_crecv.at[j // 3],
                  along_col(-SHIFTS[j]))
 
-    def halves(v):
-        return v[:, :LANES] + v[:, LANES:]
-
-    def share_rows(slot, values, sem):
+    lane = lax.broadcasted_iota(jnp.int32, (1, LANES), 1)
+    z, core = a // 2, a % 2
+    ys = [(y + d) % 4 for d in range(4)]
+    xs = [(x + d) % 4 for d in range(4)]
+    cores = [core, 1 - core]
+
+    def share(slot, values):
+        line = jnp.zeros((1, LANES), F32)
         for i, v in enumerate(values):
-            sc_out[slot, :, i * LANES:(i + 1) * LANES] = halves(v)
-        for j in range(1, NB):
-            send(sc_out.at[slot], sc_in.at[slot, j], small_send.at[sem], small_recv.at[sem],
-                 along_row(j, -1))
-
-    def summed(slot, sem):
-        settle(sc_in.at[slot, pl.ds(1, NB - 1)], small_recv.at[sem])
-        total = sc_out[slot]
-        for j in range(1, NB):
-            total = total + sc_in[slot, j]
-        return total
-
-    def share_cols(slot, total, sem):
-        sc_out[slot] = total
-        for s in range(1, NB):
-            send(sc_out.at[slot], sc_in.at[slot, s], small_send.at[sem], small_recv.at[sem],
-                 along_col(-s))
-
-    def scalars(total):
-        return [jnp.sum(total[:, i * LANES:(i + 1) * LANES], axis=1, keepdims=True)
-                for i in range(3)]
-
-    share_rows(0, (t * t, t * off, off * off), 8)
-
-    settle(o_col.at[pl.ds(1, NC - 1)], small_recv.at[7])
+            line = jnp.where(lane == i, jnp.sum(v, axis=1, keepdims=True), line)
+        sc_out[slot] = line
+
+        def plane(q, last):
+            far = 4 + (1 - 2 * (q % 2)) * ((q + 1) // 2)
+            base = ((z + far) % 8) * 4
+            for i, (dy, dx, dc) in enumerate(NEAREST_LAST):
+                if last and (dy, dx, dc) == (0, 0, 0):
+                    continue
+                where = ((base + ys[dy]) * 2 + xs[dx] // 2, (xs[dx] % 2) * 2 + cores[dc])
+                send(sc_out.at[slot], sc_in.at[slot, q * 32 + i], small_send.at[8 + slot],
+                     small_recv.at[8 + slot], where)
+
+        def one(q, carry):
+            plane(q, False)
+            return carry
+
+        lax.fori_loop(0, 7, one, 0)
+        plane(7, True)
+
+    def shared(slot):
+        settle(sc_in.at[slot, pl.ds(0, 255)], small_recv.at[8 + slot])
+        sums = [sc_out[slot]] + [sc_in[slot, i] for i in range(255)]
+        while len(sums) > 1:
+            sums = [p + q for p, q in zip(sums[::2], sums[1::2])] + sums[len(sums) & ~1:]
+        return [sums[0][:, i:i + 1] for i in range(3)]
+
+    share(0, (t * t, t * off, off * off))
+
+    for c in range(3):
+        settle(span(o_col, c, 3), o_crecv.at[c])
     lane_v = [jnp.broadcast_to(o_col[l * LANES // BLK, :, (l * LANES) % BLK:(l * LANES) % BLK + LANES],
                                (8, LANES)) for l in range(2, 16)]
     downs = tuple(jnp.zeros((8, LANES), F32) for _ in range(COLS // LANES))
     TAKE = 64
     for r in range(4):
-        lo = max(4 * r, 1)
-        settle(o_row.at[pl.ds(lo, 4 * r + 4 - lo)], o_rrecv.at[r])
+        settle(span(o_row, r, 4), o_rrecv.at[r])
         for j in range(4 * r, 4 * r + 4):
             spread(o_row[j], j)
 
@@ -295,8 +325,6 @@
         downs = lax.fori_loop(0, CHUNK // TAKE, some, downs)
         fold_rows(r, rp2)
         send_rows(r, rp2, rr2, 4)
-        if r == 2:
-            share_cols(1, summed(0, 8), 9)
 
     for k in range(NC):
         cp2[k] = jnp.concatenate([jnp.sum(downs[2 * k], axis=0, keepdims=True),
@@ -309,15 +337,14 @@
     for k in range(NC):
         quad = quad + o_col[k] * cp2[k]
 
-    s0, s1, s2 = scalars(summed(1, 9))
+    s0, s1, s2 = shared(0)
     below = DIAG * s0 + s1
     alpha = s0 / below
     gamma = s1 / below
     resid = gamma * t - alpha * off
-    share_rows(2, (resid * resid, resid * t, quad), 10)
+    share(1, (resid * resid, resid * t, quad))
     product = gathered(rp2, rr2, cp2, cr2, False) - off
-    share_cols(3, summed(2, 10), 11)
-    n1, cross, s3 = scalars(summed(3, 11))
+    n1, cross, s3 = shared(1)
     beta = n1 / s0
     both = gamma + beta
     length = n1 + 2.0 * beta * cross + beta * beta * s0
@@ -326,8 +353,10 @@
     step2 = n1 / energy
     direction = resid + beta * t
     image = DIAG * direction + both * off - alpha * product
-    sol_ref[...] = alpha * t + step2 * direction
-    res_ref[...] = resid - step2 * image
+    out_ref[0] = alpha * t
+    out_ref[1] = step2 * direction
+    out_ref[2] = resid
+    out_ref[3] = step2 * image
 
     settle(t_row.at[pl.ds(1, NB - 1)], small_send.at[0])
     settle(t_col.at[pl.ds(1, NC - 1)], small_send.at[1])
@@ -339,20 +368,19 @@
     settle(cr2.at[pl.ds(1, NC - 1)], small_send.at[5])
     settle(o_row.at[pl.ds(1, NB - 1)], small_send.at[6])
     settle(o_col.at[pl.ds(1, NC - 1)], small_send.at[7])
-    for slot in range(4):
-        settle(sc_in.at[slot, pl.ds(1, NB - 1)], small_send.at[8 + slot])
+    for slot in range(2):
+        settle(sc_in.at[slot, pl.ds(0, 255)], small_send.at[8 + slot])
 
 
 def on_device(features, projection, targets):
     vm = pl.BlockSpec(memory_space=pltpu.VMEM)
     hbm = pl.BlockSpec(memory_space=pl.ANY)
-    flat = jax.ShapeDtypeStruct((1, BLK), F32)
     dma = pltpu.SemaphoreType.DMA
-    sol, res = pl.pallas_call(
+    terms = pl.pallas_call(
         body,
-        out_shape=(flat, flat),
+        out_shape=jax.ShapeDtypeStruct((4, 1, BLK), F32),
         in_specs=[hbm, hbm, vm],
-        out_specs=(vm, vm),
+        out_specs=vm,
         scratch_shapes=[
             pltpu.VMEM((BLK, 2048), BF16), pltpu.VMEM((PROJ, 2048), BF16),
             pltpu.VMEM((NB, PROJ, BLK), F32), pltpu.VMEM((NC, PROJ, BLK), F32),
@@ -365,15 +393,16 @@
             pltpu.VMEM((NB, 1, BLK), F32), pltpu.VMEM((NC, 1, BLK), F32),
             pltpu.VMEM((NB, 1, BLK), F32), pltpu.VMEM((NC, 1, BLK), F32),
             pltpu.VMEM((NB, 1, BLK), F32), pltpu.VMEM((NC, 1, BLK), F32),
-            pltpu.VMEM((4, 1, 3 * LANES), F32), pltpu.VMEM((4, NB, 1, 3 * LANES), F32),
+            pltpu.VMEM((2, 1, LANES), F32), pltpu.VMEM((2, 256, 1, LANES), F32),
             dma((2,)), dma((2,)), dma((NB,)), dma((NC,)),
-            dma((12,)), dma((12,)), dma((4,)),
+            dma((10,)), dma((10,)), dma((4,)), dma((3,)), dma((4,)), dma((3,)),
         ],
         compiler_params=pltpu.CompilerParams(
             collective_id=0, has_side_effects=True, vmem_limit_bytes=60 * 2**20),
         name="conjugate",
     )(features, projection.T, targets.reshape(1, BLK))
-    return sol.reshape(BLK), res.reshape(BLK)
+    terms = terms.reshape(4, BLK)
+    return terms[0] + terms[1], terms[2] - terms[3]
 
 
 def solution(mesh):

time: 58.9 us -> 55.4 us (0.941)
  Pallas kernels: 56.3 us -> 53.3 us
  local copies, waits for them, and re-layouts: 1.86 us -> 0 us
  other arithmetic: 0 us -> 1.26 us
    pallas_call x1, Pallas kernels: 56.3 us -> 53.3 us  [on_device(): pl.pallas_call(body, out_shape=jax.ShapeDtypeStruct((4, 1, BLK), F32), in...]
    unnamed x6 -> x0, local copies, waits for them, and re-layouts: 1.86 us -> none
    sub x0 -> x1, other arithmetic: none -> 1.26 us  [on_device(): return (terms[0] + terms[1], terms[2] - terms[3])]
where the time goes in v2:
time: 55.4 us; the launch traced here: 55.2 us
  Pallas kernels  53.3 us (96%)
  other arithmetic  1.26 us (2%)
  between operations  0.64 us (1%)
    pallas_call x1, Pallas kernels, on_device(): pl.pallas_call(body, out_shape=jax.ShapeDtypeStruct((4, 1, BLK), F32), in...  53.3 us
    sub x1, other arithmetic, on_device(): return (terms[0] + terms[1], terms[2] - terms[3])  1.26 us

profile of v2, /device:TPU:1, one launch (start us, length us, event | category | flops | bytes accessed | tf_op | source)
XLA Modules:
  0.0 55.2 jit_solution(5184061706582037469)
XLA Ops:
  0.6 53.3 %conjugate.1 = f32[4,1,256]{2,1,0:T(1,128)} custom-call(bf16[256,2048]{1,0:T(8,128)(2,1)} %feat_hbm.1, bf16[32,2048]{1,0:T(8,128)(2,1)} %bitcast.4, f32[1,256]{1,0:T(1,128)} %bitcast.7), custom_call_target="tpu_custom_call" | custom-call | tf_op jit(solution)/shard_map/conjugate/pallas_call | solution.py:379
  54.0 1.3 %slice_subtract_fusion = (f32[1,1,256]{2,1,0:T(1,128)}, f32[1,1,256]{2,1,0:T(1,128)}) fusion(f32[4,1,256]{2,1,0:T(1,128)} %conjugate.1), kind=kLoop, calls=%fused_computation | loop fusion | flops 512 | bytes 6144 | tf_op jit(solution)/shard_map/sub | solution.py:405

commit v3 on v2

--- a/solution.py
+++ b/solution.py
@@ -55,7 +55,7 @@
          feat, proj, lat_row, lat_col, t_row, t_col, o_row, o_col,
          side_a, side_b, wide_u, tiles, row_acc, col_acc,
          rp1, cp1, rr1, cr1, rp2, cp2, rr2, cr2,
-         sc_out, sc_in, load_sem, lat_send, lat_rrecv, lat_crecv,
+         sc_out, sc_in, rs_in, cs_in, load_sem, lat_send, lat_rrecv, lat_crecv,
          small_send, small_recv, t_rrecv, t_crecv, o_rrecv, o_crecv):
     a, y, x = place()
 
@@ -80,10 +80,11 @@
     load_p.start()
 
     barrier = pltpu.get_barrier_semaphore()
-    for j in range(1, NB):
+    for j in range(NB - 1, 0, -1):
         pl.semaphore_signal(barrier, inc=1, device_id=along_row(j, 1), device_id_type=MESH)
-    for s in range(1, 16):
-        pl.semaphore_signal(barrier, inc=1, device_id=along_col(s), device_id_type=MESH)
+        if j < NC:
+            pl.semaphore_signal(barrier, inc=1, device_id=along_col(SHIFTS[j]),
+                                device_id_type=MESH)
     t_row[0] = targ_ref[...]
     t_col[0] = targ_ref[...]
     def spread(values, j):
@@ -133,7 +134,7 @@
     build_a(0)
     build_b(0)
     spread(t_row[0], 0)
-    pl.semaphore_wait(barrier, 30)
+    pl.semaphore_wait(barrier, NB + NC - 2)
 
     for j in range(1, NB):
         send(targ_ref, t_row.at[j], small_send.at[0], t_rrecv.at[j // 4], along_row(j, -1))
@@ -173,11 +174,11 @@
         near = slots(i, width)
         return ref.at[pl.ds(near[0], len(near))]
 
-    def step(r, c):
-        first_r, first_c = r not in seen_r, c not in seen_c
-        seen_r.add(r)
+    def step(low, high, c):
+        fresh, first_c = [r for r in range(low, high) if r not in seen_r], c not in seen_c
+        seen_r.update(fresh)
         seen_c.add(c)
-        if first_r:
+        for r in fresh:
             settle(span(t_row, r, 4), t_rrecv.at[r])
             for j in slots(r, 4):
                 spread(t_row[j], j)
@@ -186,11 +187,11 @@
             for k in slots(c, 3):
                 settle(lat_col.at[k], lat_crecv.at[k])
                 build_b(k)
-        if first_r:
+        for r in fresh:
             for j in slots(r, 4):
                 settle(lat_row.at[j], lat_rrecv.at[j])
                 build_a(j)
-        rows = slice(r * CHUNK, (r + 1) * CHUNK)
+        rows = slice(low * CHUNK, high * CHUNK)
         cols = slice(c * GROUP, (c + 1) * GROUP)
         power = jnp.dot(side_a[rows, :], side_b[:, cols], preferred_element_type=F32)
         p = jnp.exp2(power)
@@ -201,7 +202,7 @@
             lane = c * GROUP + i * LANES
             k = lane // BLK
             piece = p[:, i * LANES:(i + 1) * LANES]
-            down = jnp.sum((piece * u).reshape(CHUNK // 8, 8, LANES), axis=0)
+            down = jnp.sum((piece * u).reshape((high - low) * CHUNK // 8, 8, LANES), axis=0)
             if first_c:
                 col_acc[:, lane:lane + LANES] = down
             else:
@@ -209,7 +210,7 @@
             if k not in (0, NC - 1):
                 v = t_col[k, :, (lane % BLK):(lane % BLK) + LANES]
                 total = piece * v if total is None else total + piece * v
-        if first_r:
+        if fresh:
             row_acc[rows, :] = total
         else:
             row_acc[rows, :] += total
@@ -218,21 +219,17 @@
         for k in ks:
             out[k] = jnp.sum(col_acc[:, k * BLK:(k + 1) * BLK], axis=0, keepdims=True)
 
-    def finish(order, i):
-        r, c = order[i]
+    order = ((0, 1, 0), (1, 2, 0), (2, 3, 0), (3, 4, 0), (0, 2, 1), (2, 4, 1), (2, 4, 2), (1, 2, 2), (0, 1, 2))
+    for i, (low, high, c) in enumerate(order):
+        step(low, high, c)
         later = order[i + 1:]
-        return (all(r != q for q, _ in later), all(c != q for _, q in later))
-
-    order = ((0, 0), (1, 0), (2, 0), (3, 0), (0, 1), (1, 1), (2, 1), (3, 1), (0, 2), (1, 2), (2, 2), (3, 2))
-    for i, (r, c) in enumerate(order):
-        step(r, c)
-        end_r, end_c = finish(order, i)
-        if end_c:
+        if all(q != c for _, _, q in later):
             fold_cols(range(3 * c, 3 * c + 3), cp1)
             send_cols(range(3 * c, 3 * c + 3), cp1, cr1, 3)
-        if end_r:
-            fold_rows(r, rp1)
-            send_rows(r, rp1, rr1, 2)
+        for r in range(low, high):
+            if all(not l <= r < h for l, h, _ in later):
+                fold_rows(r, rp1)
+                send_rows(r, rp1, rr1, 2)
 
     def gathered(rp, rr, cp, cr, own):
         settle(rr.at[pl.ds(1, NB - 1)], small_recv.at[2 if own else 4])
@@ -254,7 +251,7 @@
     for j in range(1, NB):
         send(o_row.at[0], o_row.at[j], small_send.at[6], o_rrecv.at[j // 4], along_row(j, -1))
         if j < NC:
-            send(o_col.at[0], o_col.at[j], small_send.at[7], o_crecv.at[j // 3],
+            send(o_col.at[0], o_col.at[j], small_send.at[7], o_crecv.at[j // 5],
                  along_col(-SHIFTS[j]))
 
     lane = lax.broadcasted_iota(jnp.int32, (1, LANES), 1)
@@ -263,11 +260,23 @@
     xs = [(x + d) % 4 for d in range(4)]
     cores = [core, 1 - core]
 
-    def share(slot, values):
+    def across(v):
+        return jnp.sum(v, axis=1, keepdims=True)
+
+    def packed(values):
         line = jnp.zeros((1, LANES), F32)
         for i, v in enumerate(values):
-            line = jnp.where(lane == i, jnp.sum(v, axis=1, keepdims=True), line)
-        sc_out[slot] = line
+            line = jnp.where(lane == i, v, line)
+        return line
+
+    def added(first, ref, many):
+        sums = [first] + [ref[i] for i in range(many)]
+        while len(sums) > 1:
+            sums = [p + q for p, q in zip(sums[::2], sums[1::2])] + sums[len(sums) & ~1:]
+        return sums[0]
+
+    def share(values):
+        sc_out[0] = packed(values)
 
         def plane(q, last):
             far = 4 + (1 - 2 * (q % 2)) * ((q + 1) // 2)
@@ -276,8 +285,8 @@
                 if last and (dy, dx, dc) == (0, 0, 0):
                     continue
                 where = ((base + ys[dy]) * 2 + xs[dx] // 2, (xs[dx] % 2) * 2 + cores[dc])
-                send(sc_out.at[slot], sc_in.at[slot, q * 32 + i], small_send.at[8 + slot],
-                     small_recv.at[8 + slot], where)
+                send(sc_out.at[0], sc_in.at[q * 32 + i], small_send.at[8],
+                     small_recv.at[8], where)
 
         def one(q, carry):
             plane(q, False)
@@ -286,65 +295,115 @@
         lax.fori_loop(0, 7, one, 0)
         plane(7, True)
 
-    def shared(slot):
-        settle(sc_in.at[slot, pl.ds(0, 255)], small_recv.at[8 + slot])
-        sums = [sc_out[slot]] + [sc_in[slot, i] for i in range(255)]
-        while len(sums) > 1:
-            sums = [p + q for p, q in zip(sums[::2], sums[1::2])] + sums[len(sums) & ~1:]
-        return [sums[0][:, i:i + 1] for i in range(3)]
-
-    share(0, (t * t, t * off, off * off))
-
-    for c in range(3):
-        settle(span(o_col, c, 3), o_crecv.at[c])
-    lane_v = [jnp.broadcast_to(o_col[l * LANES // BLK, :, (l * LANES) % BLK:(l * LANES) % BLK + LANES],
-                               (8, LANES)) for l in range(2, 16)]
-    downs = tuple(jnp.zeros((8, LANES), F32) for _ in range(COLS // LANES))
+    def shared():
+        settle(sc_in.at[pl.ds(0, 255)], small_recv.at[8])
+        return added(sc_out[0], sc_in, 255)
+
+    share((across(t * t), across(t * off), across(off * off)))
+
     TAKE = 64
-    for r in range(4):
+    every = range(COLS // LANES)
+    near, far = every[:10], every[10:]
+    lane_v, downs = {}, {}
+
+    def look(lanes):
+        for l in lanes:
+            downs[l] = jnp.zeros((8, LANES), F32)
+            if 2 <= l < 16:
+                lane_v[l] = jnp.broadcast_to(
+                    o_col[l // 2, :, (l % 2) * LANES:(l % 2) * LANES + LANES], (8, LANES))
+
+    def sweep(r, lanes, first):
+        def some(i, carry):
+            start = pl.multiple_of(r * CHUNK + i * TAKE, TAKE)
+            carry = list(carry)
+            for g in range(TAKE // 8):
+                at = pl.ds(start + g * 8, 8)
+                u = wide_u[at, :]
+                total = None if first else row_acc[at, :]
+                for n, l in enumerate(lanes):
+                    piece = tiles[at, l * LANES:(l + 1) * LANES]
+                    carry[n] = carry[n] + piece * u
+                    if l in lane_v:
+                        w = piece * lane_v[l]
+                        total = w if total is None else total + w
+                row_acc[at, :] = total
+            return tuple(carry)
+
+        done = lax.fori_loop(0, CHUNK // TAKE, some, tuple(downs[l] for l in lanes))
+        downs.update(zip(lanes, done))
+
+    def arrive(r):
         settle(span(o_row, r, 4), o_rrecv.at[r])
         for j in range(4 * r, 4 * r + 4):
             spread(o_row[j], j)
 
-        def some(i, downs):
-            start = pl.multiple_of(r * CHUNK + i * TAKE, TAKE)
-            downs = list(downs)
-            for g in range(TAKE // 8):
-                at = pl.ds(start + g * 8, 8)
-                u = wide_u[at, :]
-                total = None
-                for l in range(COLS // LANES):
-                    piece = tiles[at, l * LANES:(l + 1) * LANES]
-                    downs[l] = downs[l] + piece * u
-                    if 2 <= l < 16:
-                        w = piece * lane_v[l - 2]
-                        total = w if total is None else total + w
-                row_acc[at, :] = total
-            return tuple(downs)
-
-        downs = lax.fori_loop(0, CHUNK // TAKE, some, downs)
+    quad = jnp.zeros((1, BLK), F32)
+
+    def leave(r, quad):
         fold_rows(r, rp2)
         send_rows(r, rp2, rr2, 4)
-
+        for j in range(4 * r, 4 * r + 4):
+            quad = quad + o_row[j] * rp2[j]
+        return quad
+
+    settle(o_col.at[pl.ds(1, 4)], o_crecv.at[0])
+    look(near)
+    arrive(0)
+    sweep(0, near, True)
+    arrive(1)
+    sweep(1, near, True)
+    settle(o_col.at[pl.ds(5, 4)], o_crecv.at[1])
+    look(far)
+    sweep(0, far, False)
+    quad = leave(0, quad)
+    sweep(1, far, False)
+    quad = leave(1, quad)
+    arrive(2)
+    sweep(2, every, True)
+    quad = leave(2, quad)
+    arrive(3)
+
+    total = shared()
+    s0, s1, s2 = (total[:, i:i + 1] for i in range(3))
+    below = DIAG * s0 + s1
+    alpha = s0 / below
+    gamma = s1 / below
+    resid = gamma * t - alpha * off
+    norm_own, cross_own = across(resid * resid), across(resid * t)
+
+    sweep(3, every, True)
     for k in range(NC):
         cp2[k] = jnp.concatenate([jnp.sum(downs[2 * k], axis=0, keepdims=True),
                                   jnp.sum(downs[2 * k + 1], axis=0, keepdims=True)], axis=1)
     send_cols(range(NC), cp2, cr2, 5)
-
-    quad = jnp.zeros((1, BLK), F32)
-    for j in range(NB):
-        quad = quad + o_row[j] * rp2[j]
+    quad = leave(3, quad)
     for k in range(NC):
         quad = quad + o_col[k] * cp2[k]
-
-    s0, s1, s2 = shared(0)
-    below = DIAG * s0 + s1
-    alpha = s0 / below
-    gamma = s1 / below
-    resid = gamma * t - alpha * off
-    share(1, (resid * resid, resid * t, quad))
+    sc_out[1] = packed((norm_own, cross_own, across(quad)))
+    for j in range(1, NB):
+        send(sc_out.at[1], rs_in.at[j - 1], small_send.at[9], small_recv.at[9], along_row(j, -1))
+    settle(t_row.at[pl.ds(1, NB - 1)], small_send.at[0])
+    settle(t_col.at[pl.ds(1, NC - 1)], small_send.at[1])
+    settle(lat_row.at[pl.ds(1, NB - 1)], lat_send.at[0])
+    settle(lat_col.at[pl.ds(1, NC - 1)], lat_send.at[1])
+    settle(rr1.at[pl.ds(1, NB - 1)], small_send.at[2])
+    settle(cr1.at[pl.ds(1, NC - 1)], small_send.at[3])
+    settle(rr2.at[pl.ds(1, NB - 1)], small_send.at[4])
+    settle(cr2.at[pl.ds(1, NC - 1)], small_send.at[5])
+    settle(o_row.at[pl.ds(1, NB - 1)], small_send.at[6])
+    settle(o_col.at[pl.ds(1, NC - 1)], small_send.at[7])
+    settle(sc_in.at[pl.ds(0, 255)], small_send.at[8])
+    settle(rs_in, small_recv.at[9])
+    sc_out[2] = added(sc_out[1], rs_in, NB - 1)
+    for i in range(1, NB):
+        send(sc_out.at[2], cs_in.at[i - 1], small_send.at[10], small_recv.at[10], along_col(-i))
     product = gathered(rp2, rr2, cp2, cr2, False) - off
-    n1, cross, s3 = shared(1)
+    settle(rs_in, small_send.at[9])
+    settle(cs_in, small_send.at[10])
+    settle(cs_in, small_recv.at[10])
+    total = added(sc_out[2], cs_in, NB - 1)
+    n1, cross, s3 = (total[:, i:i + 1] for i in range(3))
     beta = n1 / s0
     both = gamma + beta
     length = n1 + 2.0 * beta * cross + beta * beta * s0
@@ -358,19 +417,6 @@
     out_ref[2] = resid
     out_ref[3] = step2 * image
 
-    settle(t_row.at[pl.ds(1, NB - 1)], small_send.at[0])
-    settle(t_col.at[pl.ds(1, NC - 1)], small_send.at[1])
-    settle(lat_row.at[pl.ds(1, NB - 1)], lat_send.at[0])
-    settle(lat_col.at[pl.ds(1, NC - 1)], lat_send.at[1])
-    settle(rr1.at[pl.ds(1, NB - 1)], small_send.at[2])
-    settle(cr1.at[pl.ds(1, NC - 1)], small_send.at[3])
-    settle(rr2.at[pl.ds(1, NB - 1)], small_send.at[4])
-    settle(cr2.at[pl.ds(1, NC - 1)], small_send.at[5])
-    settle(o_row.at[pl.ds(1, NB - 1)], small_send.at[6])
-    settle(o_col.at[pl.ds(1, NC - 1)], small_send.at[7])
-    for slot in range(2):
-        settle(sc_in.at[slot, pl.ds(0, 255)], small_send.at[8 + slot])
-
 
 def on_device(features, projection, targets):
     vm = pl.BlockSpec(memory_space=pltpu.VMEM)
@@ -393,9 +439,10 @@
             pltpu.VMEM((NB, 1, BLK), F32), pltpu.VMEM((NC, 1, BLK), F32),
             pltpu.VMEM((NB, 1, BLK), F32), pltpu.VMEM((NC, 1, BLK), F32),
             pltpu.VMEM((NB, 1, BLK), F32), pltpu.VMEM((NC, 1, BLK), F32),
-            pltpu.VMEM((2, 1, LANES), F32), pltpu.VMEM((2, 256, 1, LANES), F32),
+            pltpu.VMEM((3, 1, LANES), F32), pltpu.VMEM((255, 1, LANES), F32),
+            pltpu.VMEM((NB - 1, 1, LANES), F32), pltpu.VMEM((NB - 1, 1, LANES), F32),
             dma((2,)), dma((2,)), dma((NB,)), dma((NC,)),
-            dma((10,)), dma((10,)), dma((4,)), dma((3,)), dma((4,)), dma((3,)),
+            dma((11,)), dma((11,)), dma((4,)), dma((3,)), dma((4,)), dma((2,)),
         ],
         compiler_params=pltpu.CompilerParams(
             collective_id=0, has_side_effects=True, vmem_limit_bytes=60 * 2**20),

time: 55.4 us -> 56 us (1.011)
  Pallas kernels: 53.3 us -> 53.9 us
    pallas_call x1, Pallas kernels: 53.3 us -> 53.9 us  [on_device(): pl.pallas_call(body, out_shape=jax.ShapeDtypeStruct((4, 1, BLK), F32), in...]
where the time goes in v3:
time: 56 us; the launch traced here: 55.8 us
  Pallas kernels  53.9 us (96%)
  other arithmetic  1.26 us (2%)
  between operations  0.64 us (1%)
    pallas_call x1, Pallas kernels, on_device(): pl.pallas_call(body, out_shape=jax.ShapeDtypeStruct((4, 1, BLK), F32), in...  53.9 us
    sub x1, other arithmetic, on_device(): return (terms[0] + terms[1], terms[2] - terms[3])  1.26 us

profile of v3, /device:TPU:1, one launch (start us, length us, event | category | flops | bytes accessed | tf_op | source)
XLA Modules:
  0.0 55.8 jit_solution(14310672128928341814)
XLA Ops:
  0.6 53.9 %conjugate.1 = f32[4,1,256]{2,1,0:T(1,128)} custom-call(bf16[256,2048]{1,0:T(8,128)(2,1)} %feat_hbm.1, bf16[32,2048]{1,0:T(8,128)(2,1)} %bitcast.4, f32[1,256]{1,0:T(1,128)} %bitcast.7), custom_call_target="tpu_custom_call" | custom-call | tf_op jit(solution)/shard_map/conjugate/pallas_call | solution.py:425
  54.6 1.3 %slice_subtract_fusion = (f32[1,1,256]{2,1,0:T(1,128)}, f32[1,1,256]{2,1,0:T(1,128)}) fusion(f32[4,1,256]{2,1,0:T(1,128)} %conjugate.1), kind=kLoop, calls=%fused_computation | loop fusion | flops 512 | bytes 6144 | tf_op jit(solution)/shard_map/sub | solution.py:452

commit v4 on v3

--- a/solution.py
+++ b/solution.py
@@ -55,7 +55,7 @@
          feat, proj, lat_row, lat_col, t_row, t_col, o_row, o_col,
          side_a, side_b, wide_u, tiles, row_acc, col_acc,
          rp1, cp1, rr1, cr1, rp2, cp2, rr2, cr2,
-         sc_out, sc_in, rs_in, cs_in, load_sem, lat_send, lat_rrecv, lat_crecv,
+         sc_out, sc_in, load_sem, lat_send, lat_rrecv, lat_crecv,
          small_send, small_recv, t_rrecv, t_crecv, o_rrecv, o_crecv):
     a, y, x = place()
 
@@ -131,9 +131,6 @@
     latent = lax.dot_general(proj[...], feat[...], (((1,), (1,)), ((), ())),
                              preferred_element_type=F32)
     lat_row[0] = latent * SCALE
-    build_a(0)
-    build_b(0)
-    spread(t_row[0], 0)
     pl.semaphore_wait(barrier, NB + NC - 2)
 
     for j in range(1, NB):
@@ -146,6 +143,10 @@
              along_col(-SHIFTS[j]))
     for j in range(1, NB):
         send(lat_row.at[0], lat_row.at[j], lat_send.at[0], lat_rrecv.at[j], along_row(j, -1))
+
+    build_a(0)
+    build_b(0)
+    spread(t_row[0], 0)
 
     def fold_rows(r, out):
         for i in range(CHUNK // LANES):
@@ -263,20 +264,11 @@
     def across(v):
         return jnp.sum(v, axis=1, keepdims=True)
 
-    def packed(values):
+    def share(slot, values, between=None):
         line = jnp.zeros((1, LANES), F32)
         for i, v in enumerate(values):
             line = jnp.where(lane == i, v, line)
-        return line
-
-    def added(first, ref, many):
-        sums = [first] + [ref[i] for i in range(many)]
-        while len(sums) > 1:
-            sums = [p + q for p, q in zip(sums[::2], sums[1::2])] + sums[len(sums) & ~1:]
-        return sums[0]
-
-    def share(values):
-        sc_out[0] = packed(values)
+        sc_out[slot] = line
 
         def plane(q, last):
             far = 4 + (1 - 2 * (q % 2)) * ((q + 1) // 2)
@@ -285,21 +277,27 @@
                 if last and (dy, dx, dc) == (0, 0, 0):
                     continue
                 where = ((base + ys[dy]) * 2 + xs[dx] // 2, (xs[dx] % 2) * 2 + cores[dc])
-                send(sc_out.at[0], sc_in.at[q * 32 + i], small_send.at[8],
-                     small_recv.at[8], where)
+                send(sc_out.at[slot], sc_in.at[slot, q * 32 + i], small_send.at[8 + slot],
+                     small_recv.at[8 + slot], where)
 
         def one(q, carry):
             plane(q, False)
             return carry
 
-        lax.fori_loop(0, 7, one, 0)
+        lax.fori_loop(0, 4, one, 0)
+        if between is not None:
+            between()
+        lax.fori_loop(4, 7, one, 0)
         plane(7, True)
 
-    def shared():
-        settle(sc_in.at[pl.ds(0, 255)], small_recv.at[8])
-        return added(sc_out[0], sc_in, 255)
-
-    share((across(t * t), across(t * off), across(off * off)))
+    def shared(slot):
+        settle(sc_in.at[slot, pl.ds(0, 255)], small_recv.at[8 + slot])
+        sums = [sc_out[slot]] + [sc_in[slot, i] for i in range(255)]
+        while len(sums) > 1:
+            sums = [p + q for p, q in zip(sums[::2], sums[1::2])] + sums[len(sums) & ~1:]
+        return [sums[0][:, i:i + 1] for i in range(3)]
+
+    share(0, (across(t * t), across(t * off), across(off * off)))
 
     TAKE = 64
     every = range(COLS // LANES)
@@ -342,7 +340,8 @@
 
     def leave(r, quad):
         fold_rows(r, rp2)
-        send_rows(r, rp2, rr2, 4)
+        if r < 3:
+            send_rows(r, rp2, rr2, 4)
         for j in range(4 * r, 4 * r + 4):
             quad = quad + o_row[j] * rp2[j]
         return quad
@@ -364,8 +363,7 @@
     quad = leave(2, quad)
     arrive(3)
 
-    total = shared()
-    s0, s1, s2 = (total[:, i:i + 1] for i in range(3))
+    s0, s1, s2 = shared(0)
     below = DIAG * s0 + s1
     alpha = s0 / below
     gamma = s1 / below
@@ -376,13 +374,16 @@
     for k in range(NC):
         cp2[k] = jnp.concatenate([jnp.sum(downs[2 * k], axis=0, keepdims=True),
                                   jnp.sum(downs[2 * k + 1], axis=0, keepdims=True)], axis=1)
-    send_cols(range(NC), cp2, cr2, 5)
     quad = leave(3, quad)
     for k in range(NC):
         quad = quad + o_col[k] * cp2[k]
-    sc_out[1] = packed((norm_own, cross_own, across(quad)))
-    for j in range(1, NB):
-        send(sc_out.at[1], rs_in.at[j - 1], small_send.at[9], small_recv.at[9], along_row(j, -1))
+
+    def last_parts():
+        send_rows(3, rp2, rr2, 4)
+        send_cols(range(NC), cp2, cr2, 5)
+
+    share(1, (norm_own, cross_own, across(quad)), last_parts)
+    product = gathered(rp2, rr2, cp2, cr2, False) - off
     settle(t_row.at[pl.ds(1, NB - 1)], small_send.at[0])
     settle(t_col.at[pl.ds(1, NC - 1)], small_send.at[1])
     settle(lat_row.at[pl.ds(1, NB - 1)], lat_send.at[0])
@@ -393,17 +394,10 @@
     settle(cr2.at[pl.ds(1, NC - 1)], small_send.at[5])
     settle(o_row.at[pl.ds(1, NB - 1)], small_send.at[6])
     settle(o_col.at[pl.ds(1, NC - 1)], small_send.at[7])
-    settle(sc_in.at[pl.ds(0, 255)], small_send.at[8])
-    settle(rs_in, small_recv.at[9])
-    sc_out[2] = added(sc_out[1], rs_in, NB - 1)
-    for i in range(1, NB):
-        send(sc_out.at[2], cs_in.at[i - 1], small_send.at[10], small_recv.at[10], along_col(-i))
-    product = gathered(rp2, rr2, cp2, cr2, False) - off
-    settle(rs_in, small_send.at[9])
-    settle(cs_in, small_send.at[10])
-    settle(cs_in, small_recv.at[10])
-    total = added(sc_out[2], cs_in, NB - 1)
-    n1, cross, s3 = (total[:, i:i + 1] for i in range(3))
+    for slot in range(2):
+        settle(sc_in.at[slot, pl.ds(0, 255)], small_send.at[8 + slot])
+
+    n1, cross, s3 = shared(1)
     beta = n1 / s0
     both = gamma + beta
     length = n1 + 2.0 * beta * cross + beta * beta * s0
@@ -439,10 +433,9 @@
             pltpu.VMEM((NB, 1, BLK), F32), pltpu.VMEM((NC, 1, BLK), F32),
             pltpu.VMEM((NB, 1, BLK), F32), pltpu.VMEM((NC, 1, BLK), F32),
             pltpu.VMEM((NB, 1, BLK), F32), pltpu.VMEM((NC, 1, BLK), F32),
-            pltpu.VMEM((3, 1, LANES), F32), pltpu.VMEM((255, 1, LANES), F32),
-            pltpu.VMEM((NB - 1, 1, LANES), F32), pltpu.VMEM((NB - 1, 1, LANES), F32),
+            pltpu.VMEM((2, 1, LANES), F32), pltpu.VMEM((2, 256, 1, LANES), F32),
             dma((2,)), dma((2,)), dma((NB,)), dma((NC,)),
-            dma((11,)), dma((11,)), dma((4,)), dma((3,)), dma((4,)), dma((2,)),
+            dma((10,)), dma((10,)), dma((4,)), dma((3,)), dma((4,)), dma((2,)),
         ],
         compiler_params=pltpu.CompilerParams(
             collective_id=0, has_side_effects=True, vmem_limit_bytes=60 * 2**20),

time: 56 us -> 54.2 us (0.968)
  Pallas kernels: 53.9 us -> 52.2 us
    pallas_call x1, Pallas kernels: 53.9 us -> 52.2 us  [on_device(): pl.pallas_call(body, out_shape=jax.ShapeDtypeStruct((4, 1, BLK), F32), in...]
where the time goes in v4:
time: 54.2 us; the launch traced here: 54.1 us
  Pallas kernels  52.2 us (96%)
  other arithmetic  1.26 us (2%)
  between operations  0.64 us (1%)
    pallas_call x1, Pallas kernels, on_device(): pl.pallas_call(body, out_shape=jax.ShapeDtypeStruct((4, 1, BLK), F32), in...  52.2 us
    sub x1, other arithmetic, on_device(): return (terms[0] + terms[1], terms[2] - terms[3])  1.26 us

profile of v4, /device:TPU:1, one launch (start us, length us, event | category | flops | bytes accessed | tf_op | source)
XLA Modules:
  0.0 54.1 jit_solution(16804756251056671515)
XLA Ops:
  0.6 52.2 %conjugate.1 = f32[4,1,256]{2,1,0:T(1,128)} custom-call(bf16[256,2048]{1,0:T(8,128)(2,1)} %feat_hbm.1, bf16[32,2048]{1,0:T(8,128)(2,1)} %bitcast.4, f32[1,256]{1,0:T(1,128)} %bitcast.7), custom_call_target="tpu_custom_call" | custom-call | tf_op jit(solution)/shard_map/conjugate/pallas_call | solution.py:419
  52.8 1.3 %slice_subtract_fusion = (f32[1,1,256]{2,1,0:T(1,128)}, f32[1,1,256]{2,1,0:T(1,128)}) fusion(f32[4,1,256]{2,1,0:T(1,128)} %conjugate.1), kind=kLoop, calls=%fused_computation | loop fusion | flops 512 | bytes 6144 | tf_op jit(solution)/shard_map/sub | solution.py:445

commit v5 on v4

--- a/solution.py
+++ b/solution.py
@@ -166,7 +166,8 @@
                 send(out.at[k], into.at[k], small_send.at[sem], small_recv.at[sem],
                      along_col(SHIFTS[k]))
 
-    seen_r, seen_c = set(), set()
+    told, ready_r, ready_c = set(), {0}, {0}
+    begun_r, begun_c = set(), set()
 
     def slots(i, width):
         return range(max(width * i, 1), width * i + width)
@@ -175,60 +176,73 @@
         near = slots(i, width)
         return ref.at[pl.ds(near[0], len(near))]
 
-    def step(low, high, c):
-        fresh, first_c = [r for r in range(low, high) if r not in seen_r], c not in seen_c
-        seen_r.update(fresh)
-        seen_c.add(c)
-        for r in fresh:
-            settle(span(t_row, r, 4), t_rrecv.at[r])
-            for j in slots(r, 4):
+    def step(low, high, left, right):
+        for j in range(low, high):
+            if ("r", j // 4) not in told:
+                told.add(("r", j // 4))
+                settle(span(t_row, j // 4, 4), t_rrecv.at[j // 4])
+        for k in range(left, right):
+            if ("c", k // 3) not in told:
+                told.add(("c", k // 3))
+                settle(span(t_col, k // 3, 3), t_crecv.at[k // 3])
+        for j in range(low, high):
+            if j not in ready_r:
                 spread(t_row[j], j)
-        if first_c:
-            settle(span(t_col, c, 3), t_crecv.at[c])
-            for k in slots(c, 3):
+        for k in range(left, right):
+            if k not in ready_c:
+                ready_c.add(k)
                 settle(lat_col.at[k], lat_crecv.at[k])
                 build_b(k)
-        for r in fresh:
-            for j in slots(r, 4):
+        for j in range(low, high):
+            if j not in ready_r:
+                ready_r.add(j)
                 settle(lat_row.at[j], lat_rrecv.at[j])
                 build_a(j)
-        rows = slice(low * CHUNK, high * CHUNK)
-        cols = slice(c * GROUP, (c + 1) * GROUP)
+        rows = slice(low * BLK, high * BLK)
+        cols = slice(left * BLK, right * BLK)
         power = jnp.dot(side_a[rows, :], side_b[:, cols], preferred_element_type=F32)
         p = jnp.exp2(power)
         tiles[rows, cols] = p
         u = wide_u[rows, :]
         total = None
-        for i in range(GROUP // LANES):
-            lane = c * GROUP + i * LANES
+        for i in range((right - left) * BLK // LANES):
+            lane = left * BLK + i * LANES
             k = lane // BLK
             piece = p[:, i * LANES:(i + 1) * LANES]
-            down = jnp.sum((piece * u).reshape((high - low) * CHUNK // 8, 8, LANES), axis=0)
-            if first_c:
+            down = jnp.sum((piece * u).reshape((high - low) * BLK // 8, 8, LANES), axis=0)
+            if k not in begun_c:
                 col_acc[:, lane:lane + LANES] = down
             else:
                 col_acc[:, lane:lane + LANES] += down
             if k not in (0, NC - 1):
                 v = t_col[k, :, (lane % BLK):(lane % BLK) + LANES]
                 total = piece * v if total is None else total + piece * v
-        if fresh:
-            row_acc[rows, :] = total
-        else:
-            row_acc[rows, :] += total
+        begun_c.update(range(left, right))
+        if total is not None:
+            if low in begun_r:
+                row_acc[rows, :] += total
+            else:
+                row_acc[rows, :] = total
+            begun_r.update(range(low, high))
 
     def fold_cols(ks, out):
         for k in ks:
             out[k] = jnp.sum(col_acc[:, k * BLK:(k + 1) * BLK], axis=0, keepdims=True)
 
-    order = ((0, 1, 0), (1, 2, 0), (2, 3, 0), (3, 4, 0), (0, 2, 1), (2, 4, 1), (2, 4, 2), (1, 2, 2), (0, 1, 2))
-    for i, (low, high, c) in enumerate(order):
-        step(low, high, c)
+    order = ((0, 4, 0, 3), (4, 8, 0, 3), (8, 12, 0, 3), (12, 14, 0, 3), (0, 4, 3, 6), (4, 8, 3, 6), (8, 14, 3, 6),
+             (0, 8, 6, 9), (8, 14, 6, 9), (14, 16, 0, 9))
+    sent_r = set()
+    for i, (low, high, left, right) in enumerate(order):
+        step(low, high, left, right)
         later = order[i + 1:]
-        if all(q != c for _, _, q in later):
-            fold_cols(range(3 * c, 3 * c + 3), cp1)
-            send_cols(range(3 * c, 3 * c + 3), cp1, cr1, 3)
-        for r in range(low, high):
-            if all(not l <= r < h for l, h, _ in later):
+        for k in range(left, right):
+            if all(not l <= k < h for _, _, l, h in later):
+                fold_cols([k], cp1)
+                send_cols([k], cp1, cr1, 3)
+        rest = [(b, e) for b, e, l, _ in later if l < NC - 1]
+        for r in range(4):
+            if r not in sent_r and all(e <= 4 * r or 4 * r + 4 <= b for b, e in rest):
+                sent_r.add(r)
                 fold_rows(r, rp1)
                 send_rows(r, rp1, rr1, 2)
 

time: 54.2 us -> 54.1 us (level)
  no operation moved by 1% of the time
where the time goes in v5:
time: 54.1 us; the launch traced here: 54 us
  Pallas kernels  52.1 us (96%)
  other arithmetic  1.26 us (2%)
  between operations  0.64 us (1%)
    pallas_call x1, Pallas kernels, on_device(): pl.pallas_call(body, out_shape=jax.ShapeDtypeStruct((4, 1, BLK), F32), in...  52.1 us
    sub x1, other arithmetic, on_device(): return (terms[0] + terms[1], terms[2] - terms[3])  1.26 us

profile of v5, /device:TPU:1, one launch (start us, length us, event | category | flops | bytes accessed | tf_op | source)
XLA Modules:
  0.0 54.0 jit_solution(3053548264049399784)
XLA Ops:
  0.6 52.1 %conjugate.1 = f32[4,1,256]{2,1,0:T(1,128)} custom-call(bf16[256,2048]{1,0:T(8,128)(2,1)} %feat_hbm.1, bf16[32,2048]{1,0:T(8,128)(2,1)} %bitcast.4, f32[1,256]{1,0:T(1,128)} %bitcast.7), custom_call_target="tpu_custom_call" | custom-call | tf_op jit(solution)/shard_map/conjugate/pallas_call | solution.py:433
  52.8 1.3 %slice_subtract_fusion = (f32[1,1,256]{2,1,0:T(1,128)}, f32[1,1,256]{2,1,0:T(1,128)}) fusion(f32[4,1,256]{2,1,0:T(1,128)} %conjugate.1), kind=kLoop, calls=%fused_computation | loop fusion | flops 512 | bytes 6144 | tf_op jit(solution)/shard_map/sub | solution.py:459

commit v6 on v5

--- a/solution.py
+++ b/solution.py
@@ -74,10 +74,13 @@
     def settle(ref, sem):
         pltpu.make_async_copy(ref, ref, sem).wait()
 
-    load_f = pltpu.make_async_copy(feat_hbm, feat, load_sem.at[0])
-    load_p = pltpu.make_async_copy(proj_hbm, proj, load_sem.at[1])
-    load_f.start()
+    halves = [pl.ds(0, 1024), pl.ds(1024, 1024)]
+    load_p = pltpu.make_async_copy(proj_hbm, proj, load_sem.at[0])
+    load_f = [pltpu.make_async_copy(feat_hbm.at[:, h], feat.at[:, h], load_sem.at[1 + i])
+              for i, h in enumerate(halves)]
     load_p.start()
+    for load in load_f:
+        load.start()
 
     barrier = pltpu.get_barrier_semaphore()
     for j in range(NB - 1, 0, -1):
@@ -127,9 +130,11 @@
             [h, m, h, m, l, h, extra(qh, qm, ql, 3), zeros], axis=0)
 
     load_p.wait()
-    load_f.wait()
-    latent = lax.dot_general(proj[...], feat[...], (((1,), (1,)), ((), ())),
-                             preferred_element_type=F32)
+    latent = jnp.zeros((PROJ, BLK), F32)
+    for load, h in zip(load_f, halves):
+        load.wait()
+        latent = latent + lax.dot_general(proj[:, h], feat[:, h], (((1,), (1,)), ((), ())),
+                                          preferred_element_type=F32)
     lat_row[0] = latent * SCALE
     pl.semaphore_wait(barrier, NB + NC - 2)
 
@@ -258,9 +263,6 @@
 
     t = targ_ref[...]
     off = gathered(rp1, rr1, cp1, cr1, True) - t
-    def halves(v):
-        return v[:, :LANES] + v[:, LANES:]
-
     o_row[0] = off
     o_col[0] = off
     for j in range(1, NB):
@@ -448,7 +450,7 @@
             pltpu.VMEM((NB, 1, BLK), F32), pltpu.VMEM((NC, 1, BLK), F32),
             pltpu.VMEM((NB, 1, BLK), F32), pltpu.VMEM((NC, 1, BLK), F32),
             pltpu.VMEM((2, 1, LANES), F32), pltpu.VMEM((2, 256, 1, LANES), F32),
-            dma((2,)), dma((2,)), dma((NB,)), dma((NC,)),
+            dma((3,)), dma((2,)), dma((NB,)), dma((NC,)),
             dma((10,)), dma((10,)), dma((4,)), dma((3,)), dma((4,)), dma((2,)),
         ],
         compiler_params=pltpu.CompilerParams(

time: 54.1 us -> 54.1 us (level)
  no operation moved by 1% of the time
where the time goes in v6:
time: 54.1 us; the launch traced here: 54 us
  Pallas kernels  52.1 us (96%)
  other arithmetic  1.26 us (2%)
  between operations  0.64 us (1%)
    pallas_call x1, Pallas kernels, on_device(): pl.pallas_call(body, out_shape=jax.ShapeDtypeStruct((4, 1, BLK), F32), in...  52.1 us
    sub x1, other arithmetic, on_device(): return (terms[0] + terms[1], terms[2] - terms[3])  1.26 us

profile of v6, /device:TPU:1, one launch (start us, length us, event | category | flops | bytes accessed | tf_op | source)
XLA Modules:
  0.0 54.0 jit_solution(15380702237030588696)
XLA Ops:
  0.6 52.1 %conjugate.1 = f32[4,1,256]{2,1,0:T(1,128)} custom-call(bf16[256,2048]{1,0:T(8,128)(2,1)} %feat_hbm.1, bf16[32,2048]{1,0:T(8,128)(2,1)} %bitcast.4, f32[1,256]{1,0:T(1,128)} %bitcast.7), custom_call_target="tpu_custom_call" | custom-call | tf_op jit(solution)/shard_map/conjugate/pallas_call | solution.py:435
  52.7 1.3 %slice_subtract_fusion = (f32[1,1,256]{2,1,0:T(1,128)}, f32[1,1,256]{2,1,0:T(1,128)}) fusion(f32[4,1,256]{2,1,0:T(1,128)} %conjugate.1), kind=kLoop, calls=%fused_computation | loop fusion | flops 512 | bytes 6144 | tf_op jit(solution)/shard_map/sub | solution.py:461

commit v7 on v6

--- a/solution.py
+++ b/solution.py
@@ -234,8 +234,8 @@
         for k in ks:
             out[k] = jnp.sum(col_acc[:, k * BLK:(k + 1) * BLK], axis=0, keepdims=True)
 
-    order = ((0, 4, 0, 3), (4, 8, 0, 3), (8, 12, 0, 3), (12, 14, 0, 3), (0, 4, 3, 6), (4, 8, 3, 6), (8, 14, 3, 6),
-             (0, 8, 6, 9), (8, 14, 6, 9), (14, 16, 0, 9))
+    order = ((0, 4, 0, 3), (4, 8, 0, 3), (8, 12, 0, 3), (0, 4, 3, 6), (4, 8, 3, 6), (8, 12, 3, 6),
+             (12, 14, 0, 6), (0, 8, 6, 8), (8, 14, 6, 8), (14, 16, 0, 8), (0, 8, 8, 9), (8, 16, 8, 9))
     sent_r = set()
     for i, (low, high, left, right) in enumerate(order):
         step(low, high, left, right)

time: 54.1 us -> 54.4 us (level)
  no operation moved by 1% of the time
where the time goes in v7:
time: 54.4 us; the launch traced here: 54.3 us
  Pallas kernels  52.4 us (96%)
  other arithmetic  1.26 us (2%)
  between operations  0.64 us (1%)
    pallas_call x1, Pallas kernels, on_device(): pl.pallas_call(body, out_shape=jax.ShapeDtypeStruct((4, 1, BLK), F32), in...  52.4 us
    sub x1, other arithmetic, on_device(): return (terms[0] + terms[1], terms[2] - terms[3])  1.26 us

profile of v7, /device:TPU:1, one launch (start us, length us, event | category | flops | bytes accessed | tf_op | source)
XLA Modules:
  0.0 54.3 jit_solution(13151088348700025807)
XLA Ops:
  0.6 52.4 %conjugate.1 = f32[4,1,256]{2,1,0:T(1,128)} custom-call(bf16[256,2048]{1,0:T(8,128)(2,1)} %feat_hbm.1, bf16[32,2048]{1,0:T(8,128)(2,1)} %bitcast.4, f32[1,256]{1,0:T(1,128)} %bitcast.7), custom_call_target="tpu_custom_call" | custom-call | tf_op jit(solution)/shard_map/conjugate/pallas_call | solution.py:435
  53.0 1.3 %slice_subtract_fusion = (f32[1,1,256]{2,1,0:T(1,128)}, f32[1,1,256]{2,1,0:T(1,128)}) fusion(f32[4,1,256]{2,1,0:T(1,128)} %conjugate.1), kind=kLoop, calls=%fused_computation | loop fusion | flops 512 | bytes 6144 | tf_op jit(solution)/shard_map/sub | solution.py:461
